TPU v7x, 128 devices: a whole 4x4x4 slice. The times are simulated.
128 devices in a mesh: point: 8 (over x, core), cent: 16 (over z, y).
Axes of the slice: x: 4, y: 4, z: 4, core: 2. Of those that a mesh axis runs over, the one named last changes fastest.
Arguments:
- points: bfloat16 [262144, 1024], P(('point', 'cent')), may hold values from -200 to 200
- cluster_ids: int32 [262144], P(('point', 'cent')), may hold values from 0 to 31, as said below
- owner_slot: int32 [32], replicated, may hold values from 0 to 31, as said below
- centroids: bfloat16 [32, 256, 1024], P('point', 'cent'), may hold values from -0.8 to 0.8
Outputs:
- new_centroids: bfloat16 [32, 256, 1024], P('point', 'cent')
- centroid_mass: float32 [32, 256], P('point', 'cent')
Inputs may be any that keep to these rules, and one draw needn't show every extreme that they name: `cluster_ids`: cluster of each point. Among the 2048 points of one device at most 128 lie in any one level-one cluster, and in every draw, for each index of cent there is one owner (point index) such that each of that owner's 4 clusters receives exactly 128 points from every device with that cent index; every other cluster receives fewer than 128 from each device. Each block row once: a permutation. Cluster c belongs to point index owner_slot[c] // 4.
All inputs are finite; a program needn't handle non-finite values.
Results may differ from a plain program's by a relative error of at most 0.0063.
Values may be sent and summed in bfloat16 or wider, within the bound.
No kernel may reach another device: no remote copies, remote signals or barrier semaphores. Data moves between devices by JAX's collectives and lax.ppermute only.
A program may use at most 128 MiB of HBM per device.

v0:
```python
import jax
import jax.numpy as jnp
from jax import lax
from jax.sharding import PartitionSpec as P

ITERS = 2
score_scale = 0.25
prior_weight = 1.0


def responsibilities(received, present, full_blocks):
    squares = jnp.sum(jnp.square(full_blocks.astype(jnp.float32)), axis=-1)
    products = jnp.einsum(
        "pjcd,jkd->pjck", received, full_blocks, preferred_element_type=jnp.float32
    )
    scores = (products - 0.5 * squares[None, :, None, :]) * score_scale
    weights = jax.nn.softmax(scores, axis=-1) * present[..., None]
    totals = jnp.einsum(
        "pjck,pjcd->jkd", weights.astype(jnp.bfloat16), received, preferred_element_type=jnp.float32
    )
    masses = jnp.sum(weights, axis=(0, 2))
    return (totals, masses)


def refine(totals, masses, centers):
    updated = (totals + prior_weight * centers.astype(jnp.float32)) / (
        masses[..., None] + prior_weight
    )
    return updated.astype(jnp.bfloat16)


def shards(points, cluster_ids, owner_slot, centroids):
    point_count = lax.axis_size("point")
    local_rows, feature_width = points.shape
    cluster_total = owner_slot.shape[0]
    per_owner = cluster_total // point_count
    capacity = 2 * local_rows // cluster_total
    cluster_table = jnp.arange(cluster_total, dtype=jnp.int32)
    member_of = cluster_ids[:, None] == cluster_table[None, :]
    block_of = jnp.sum(jnp.where(member_of, owner_slot[None, :], 0), axis=1)
    one_hot = (block_of[:, None] == cluster_table[None, :]).astype(jnp.int32)
    before = jnp.cumsum(one_hot, axis=0) - one_hot
    position = jnp.sum(before * one_hot, axis=1)
    target = block_of * capacity + position
    outgoing = (
        jnp.zeros((cluster_total * capacity, feature_width), jnp.bfloat16).at[target].set(points)
    )
    occupied = (
        jnp.zeros((cluster_total * capacity,), jnp.bfloat16)
        .at[target]
        .set(jnp.ones((local_rows,), jnp.bfloat16))
    )
    outgoing = outgoing.reshape(point_count, per_owner * capacity, feature_width)
    occupied = occupied.reshape(point_count, per_owner * capacity)
    received, arrived = (
        lax.all_to_all(outgoing, "point", split_axis=0, concat_axis=0, tiled=True),
        lax.all_to_all(occupied, "point", split_axis=0, concat_axis=0, tiled=True),
    )
    received = received.reshape(point_count, per_owner, capacity, feature_width)
    present = arrived.reshape(point_count, per_owner, capacity).astype(jnp.float32)
    own_blocks = centroids
    part_masses = jnp.zeros(centroids.shape[:2], jnp.float32)
    for iteration in range(ITERS):
        full_blocks = lax.all_gather(own_blocks, "cent", axis=1, tiled=True)
        totals, masses = responsibilities(received, present, full_blocks)
        part_totals, part_masses = (
            lax.psum_scatter(totals, "cent", scatter_dimension=1, tiled=True),
            lax.psum_scatter(masses, "cent", scatter_dimension=1, tiled=True),
        )
        own_blocks = refine(part_totals, part_masses, own_blocks)
    return (own_blocks, part_masses)


def solution(mesh):
    return jax.shard_map(
        shards,
        mesh=mesh,
        in_specs=(P(("point", "cent"), None), P(("point", "cent")), P(), P("point", "cent", None)),
        out_specs=(P("point", "cent", None), P("point", "cent")),
        check_vma=False,
    )
```

profile of v0, /device:TPU:0, one launch (start us, length us, event | category | flops | bytes accessed | tf_op | source)
XLA Modules:
  0.0 401.7 jit_solution(8172812431339845163)
XLA Ops:
  7.2 0.8 select_reduce_fusion
  8.0 9.1 %reduce-window.6 = s32[32,16,128]{2,1,0:T(8,128)S(1)} reduce-window(s32[32,16,128]{2,1,0:T(8,128)S(1)} %fusion.39, s32[]{:T(128)} %constant.11.clone.1), window={size=1x1x128 pad=0_0x0_0x127_0}, to_apply=%region_1.2 | reduce-window | flops 8323072 | bytes 524292 | tf_op jit(solution)/shard_map/reduce-window
  17.1 0.1 slice.8
  17.2 0.2 copy.36
  17.5 0.2 reduce-window.9
  17.7 0.1 broadcast_add_fusion
  17.8 0.1 fusion.38
  18.0 14.6 %scatter_custom_fusion.1 = bf16[4096]{0:T(1024)(128)(2,1)S(1)} fusion(s32[2048]{0:T(1024)S(1)} %bitcast.77, bf16[2048]{0:T(1024)(128)(2,1)S(1)} %broadcast.86, bf16[]{:T(256)} %constant.10.clone.1), kind=kCustom, calls=%fused_computation.55 | custom fusion | bytes 8194 | tf_op jit(solution)/shard_map/scatter | solution.py:51
  32.6 0.5 broadcast.108
  33.1 0.7 reduce
  33.8 0.6 reshape.117
  34.4 4.4 %all-to-all-start.1 = ((bf16[8,2,256]{2,1,0:T(2,128)(2,1)}), bf16[8,2,256]{2,1,0:T(2,128)(2,1)S(1)}, u32[]{:S(2)}, u32[]{:S(2)}) async-start(bf16[8,2,256]{2,1,0:T(2,128)(2,1)} %reshape.117), calls=%async_computation.1 | async-start | bytes 16384 | tf_op jit(solution)/shard_map/all_to_all | solution.py:57
  38.8 15.2 %scatter_custom_fusion = bf16[4096,1024]{1,0:T(8,128)(2,1)} fusion(s32[2048]{0:T(1024)S(1)} %bitcast.78, bf16[2048,1024]{1,0:T(8,128)(2,1)} %param.4, bf16[]{:T(256)} %constant.10.clone.1), kind=kCustom, calls=%fused_computation.26 | custom fusion | bytes 8389120 | tf_op jit(solution)/shard_map/scatter | solution.py:46
  54.0 0.0 all-to-all-done.1
  54.0 5.0 %all-to-all-start = ((bf16[8,512,1024]{2,1,0:T(8,128)(2,1)}), bf16[8,512,1024]{2,1,0:T(8,128)(2,1)}, u32[]{:S(2)}, u32[]{:S(2)}) async-start(bf16[8,512,1024]{2,1,0:T(8,128)(2,1)} %bitcast.71), calls=%async_computation | async-start | bytes 16777216 | tf_op jit(solution)/shard_map/all_to_all | solution.py:56
  59.0 0.0 all-gather.3.cloned.1.call-start
  59.1 0.7 all-gather.3.cloned.1.call-update
  59.7 0.2 reduce-scatter.5.cloned.1.call-start
  60.0 50.1 %all-gather.3.cloned.1.call-done = bf16[4,256,1024]{2,1,0:T(8,128)(2,1)} async-done(((bf16[4,16,1024]{2,1,0:T(8,128)(2,1)}), bf16[4,256,1024]{2,1,0:T(8,128)(2,1)}) %all-gather.3.cloned.1.call-update) | async-done | bytes 2097168 | tf_op jit(solution)/shard_map/all_gather | solution.py:64
  110.1 2.1 multiply_reduce_fusion.1
  112.2 41.4 %all-to-all-done = bf16[8,512,1024]{2,1,0:T(8,128)(2,1)} async-done(((bf16[8,512,1024]{2,1,0:T(8,128)(2,1)}), bf16[8,512,1024]{2,1,0:T(8,128)(2,1)}, u32[]{:S(2)}, u32[]{:S(2)}) %all-to-all-start) | async-done | bytes 8388640 | tf_op jit(solution)/shard_map/all_to_all | solution.py:56
  153.6 6.3 %fusion.8 = f32[4,8,128,256]{3,2,1,0:T(8,128)S(1)} fusion(bf16[8,4,128,1024]{3,2,1,0:T(8,128)(2,1)} %bitcast.7, bf16[4,256,1024]{2,1,0:T(8,128)(2,1)} %all-gather.3.cloned.1.call-done), kind=kOutput, calls=%fused_computation.10 | convolution fusion | flops 2147483648 | bytes 14680064 | tf_op jit(solution)/shard_map/pjcd,jkd->pjck/dot_general | solution.py:13
  160.0 1.8 fusion.44
  161.8 0.0 copy-start
  161.8 1.9 copy-done
  163.7 7.1 %fusion.20 = f32[4,256,1024]{2,1,0:T(8,128)} fusion(bf16[8,4,128,1024]{3,2,1,0:T(8,128)(2,1)} %bitcast.7, f32[8,4,128,256]{3,2,0,1:T(8,128)S(1)} %get-tuple-element.5, f32[8,4,128]{2,0,1:T(8,128)S(1)} %bitcast_convert_fusion, f32[8,4,128]{2,0,1:T(8,128)S(1)} %get-tuple-element.4), kind=kOutput, calls=%fused_computation.28 | convolution fusion | flops 2150629376 | bytes 16809984 | tf_op jit(solution)/shard_map/pjck,pjcd->jkd/dot_general | solution.py:18
  170.8 0.0 copy-start.4
  170.8 0.0 copy-start.3
  170.8 0.0 reduce-scatter.5.cloned.1.call-update
  170.9 0.0 all-gather.5.cloned.1.call-start
  170.9 0.6 copy-done.4
  171.5 0.6 dynamic-slice
  172.7 2.9 fusion.34
  175.6 42.3 %all-reduce = f32[4,256]{1,0:T(4,128)S(1)} all-reduce(f32[4,256]{1,0:T(4,128)S(1)} %fusion.34), channel_id=3, replica_groups=mesh['point'=8,'cent'=16] {'cent'}, use_global_device_ids=true, to_apply=%region_11.12.clone | all-reduce | flops 1024 | bytes 8192
  217.9 0.1 dynamic-slice_add_fusion
  217.9 31.4 %reduce-scatter.5.cloned.1.call-done = f32[4,16,1024]{2,1,0:T(8,128)} async-done(((f32[4,256,1024]{2,1,0:T(8,128)}), f32[4,16,1024]{2,1,0:T(8,128)}) %reduce-scatter.5.cloned.1.call-update) | async-done | bytes 262160 | tf_op jit(solution)/shard_map/reduce_scatter | solution.py:67
  249.4 0.0 copy-done.3
  249.4 1.7 divide_convert_fusion.1
  251.0 0.0 all-gather.5.cloned.1.call-update
  251.1 0.0 reduce-scatter.7.cloned.1.call-start
  251.1 45.7 %all-gather.5.cloned.1.call-done = bf16[4,256,1024]{2,1,0:T(8,128)(2,1)} async-done(((bf16[4,16,1024]{2,1,0:T(8,128)(2,1)}), bf16[4,256,1024]{2,1,0:T(8,128)(2,1)}) %all-gather.5.cloned.1.call-update) | async-done | bytes 2097168 | tf_op jit(solution)/shard_map/all_gather | solution.py:64
  296.8 2.1 multiply_reduce_fusion
  298.9 6.4 %fusion.4 = f32[4,256,8,128]{1,3,2,0:T(8,128)S(1)} fusion(bf16[8,4,128,1024]{3,2,1,0:T(8,128)(2,1)} %bitcast.7, bf16[4,256,1024]{2,1,0:T(8,128)(2,1)} %all-gather.5.cloned.1.call-done), kind=kOutput, calls=%fused_computation.6 | convolution fusion | flops 2147483648 | bytes 14680064 | tf_op jit(solution)/shard_map/pjcd,jkd->pjck/dot_general | solution.py:13
  305.3 1.8 fusion.45
  307.1 0.0 copy-start.1
  307.1 1.9 copy-done.1
  309.1 7.1 %fusion.23 = f32[4,256,1024]{2,1,0:T(8,128)} fusion(bf16[8,4,128,1024]{3,2,1,0:T(8,128)(2,1)} %bitcast.7, f32[8,4,128,256]{3,2,0,1:T(8,128)S(1)} %get-tuple-element.7, f32[8,4,128]{2,0,1:T(8,128)S(1)} %get-tuple-element.6, f32[8,4,128]{2,0,1:T(8,128)S(1)} %bitcast_convert_fusion), kind=kOutput, calls=%fused_computation.29 | convolution fusion | flops 2150629376 | bytes 16809984 | tf_op jit(solution)/shard_map/pjck,pjcd->jkd/dot_general | solution.py:18
  316.2 0.0 copy-start.2
  316.2 0.0 reduce-scatter.7.cloned.1.call-update
  316.2 2.9 fusion.35
  319.1 38.4 %all-reduce.1 = f32[4,256]{1,0:T(4,128)S(1)} all-reduce(f32[4,256]{1,0:T(4,128)S(1)} %fusion.35), channel_id=5, replica_groups=mesh['point'=8,'cent'=16] {'cent'}, use_global_device_ids=true, to_apply=%region_17.18.clone | all-reduce | flops 1024 | bytes 8192
  357.5 0.7 broadcast_add_fusion.1
  358.2 35.3 %reduce-scatter.7.cloned.1.call-done = f32[4,16,1024]{2,1,0:T(8,128)} async-done(((f32[4,256,1024]{2,1,0:T(8,128)}), f32[4,16,1024]{2,1,0:T(8,128)}) %reduce-scatter.7.cloned.1.call-update) | async-done | bytes 262160 | tf_op jit(solution)/shard_map/reduce_scatter | solution.py:67
  393.4 0.0 copy-done.2
  393.4 1.7 divide_convert_fusion
  (9 shorter events, 0.1 us)
Async XLA Ops:
  34.4 19.6 %all-to-all-start.1 = ((bf16[8,2,256]{2,1,0:T(2,128)(2,1)}), bf16[8,2,256]{2,1,0:T(2,128)(2,1)S(1)}, u32[]{:S(2)}, u32[]{:S(2)}) async-start(bf16[8,2,256]{2,1,0:T(2,128)(2,1)} %reshape.117), calls=%async_computation.1 | async-start | bytes 16384 | tf_op jit(solution)/shard_map/all_to_all | solution.py:57
  54.0 99.6 %all-to-all-start = ((bf16[8,512,1024]{2,1,0:T(8,128)(2,1)}), bf16[8,512,1024]{2,1,0:T(8,128)(2,1)}, u32[]{:S(2)}, u32[]{:S(2)}) async-start(bf16[8,512,1024]{2,1,0:T(8,128)(2,1)} %bitcast.71), calls=%async_computation | async-start | bytes 16777216 | tf_op jit(solution)/shard_map/all_to_all | solution.py:56
  59.0 51.1 %all-gather.3.cloned.1.call-start = ((), (), s32[]{:S(2)}) async-start(), calls=%async_computation.4 | async-start | bytes 2228224 | tf_op jit(solution)/shard_map/all_gather | solution.py:64
  59.7 189.6 %reduce-scatter.5.cloned.1.call-start = ((), (), s32[]{:S(2)}) async-start(), calls=%async_computation.5 | async-start | bytes 4456448 | tf_op jit(solution)/shard_map/reduce_scatter | solution.py:67
  161.8 2.0 copy-start
  170.8 0.7 copy-start.4
  170.8 78.5 %copy-start.3 = (bf16[4,16,1024]{2,1,0:T(8,128)(2,1)S(1)}, bf16[4,16,1024]{2,1,0:T(8,128)(2,1)}, u32[]{:S(2)}) copy-start(bf16[4,16,1024]{2,1,0:T(8,128)(2,1)} %param.7) | copy-start | bytes 393220
  170.9 126.0 %all-gather.5.cloned.1.call-start = ((), (), s32[]{:S(2)}) async-start(), calls=%async_computation.6 | async-start | bytes 2228224 | tf_op jit(solution)/shard_map/all_gather | solution.py:64
  251.1 142.4 %reduce-scatter.7.cloned.1.call-start = ((), (), s32[]{:S(2)}) async-start(), calls=%async_computation.7 | async-start | bytes 4456448 | tf_op jit(solution)/shard_map/reduce_scatter | solution.py:67
  307.1 2.0 copy-start.1
  316.2 77.3 %copy-start.2 = (bf16[4,16,1024]{2,1,0:T(8,128)(2,1)S(1)}, bf16[4,16,1024]{2,1,0:T(8,128)(2,1)}, u32[]{:S(2)}) copy-start(bf16[4,16,1024]{2,1,0:T(8,128)(2,1)} %divide_convert_fusion.1) | copy-start | bytes 393220
Sparse Core Ops, SparseCore 0:
  62.0 48.1 all-gather.2
  171.0 78.3 reduce-scatter.4
  252.3 44.4 all-gather.4
  316.3 77.0 reduce-scatter.6
where the time goes:
time: 402 us
  waiting for transfers between devices  205 us (51%)
  blocking collectives  80.7 us (20%)
  local copies, waits for them, and re-layouts  36.4 us (9%)
  other arithmetic  28.6 us (7%)
  matrix products  27 us (7%)
  between operations  14.6 us (4%)
  starting transfers between devices  9.69 us (2%)
    all_gather x2, waiting for transfers between devices, shards(): full_blocks = lax.all_gather(own_blocks, 'cent', axis=1, tiled=True)  95.9 us
    unnamed x2, blocking collectives  80.7 us
    reduce_scatter x2, waiting for transfers between devices, shards(): lax.psum_scatter(totals, 'cent', scatter_dimension=1, tiled=True)  66.7 us
    all_to_all x1, waiting for transfers between devices, shards(): lax.all_to_all(outgoing, 'point', split_axis=0, concat_axis=0, tiled=True)  41.4 us
    scatter x1, local copies, waits for them, and re-layouts, shards(): jnp.zeros((cluster_total * capacity, feature_width), jnp.bfloat16)  15.2 us
    scatter x1, local copies, waits for them, and re-layouts, shards(): occupied = jnp.zeros((cluster_total * capacity,), jnp.bfloat16).at[target...  14.6 us
    dot_general x2, matrix products, responsibilities(): jnp.einsum('pjck,pjcd->jkd', weights.astype(jnp.bfloat16), received, pref...  14.2 us
    dot_general x2, matrix products, responsibilities(): jnp.einsum('pjcd,jkd->pjck', received, full_blocks, preferred_element_typ...  12.7 us
  transfers between devices with their start and end apart: 6, of which 5 were waited for; matrix products, arithmetic and copies ran while one was open for 6% of the time, Pallas kernels for 0%

commit v1 on v0

--- a/solution.py
+++ b/solution.py
@@ -61,7 +61,9 @@
     own_blocks = centroids
     part_masses = jnp.zeros(centroids.shape[:2], jnp.float32)
     for iteration in range(ITERS):
-        full_blocks = lax.all_gather(own_blocks, "cent", axis=1, tiled=True)
+        full_blocks = jnp.concatenate(
+            lax.all_to_all(jnp.stack([own_blocks] * lax.axis_size("cent")), "cent", 0, 0), axis=1
+        )
         totals, masses = responsibilities(received, present, full_blocks)
         part_totals, part_masses = (
             lax.psum_scatter(totals, "cent", scatter_dimension=1, tiled=True),

time: 402 us -> 417 us (1.037)
  blocking collectives: 80.7 us -> 115 us
  waiting for transfers between devices: 205 us -> 176 us
  local copies, waits for them, and re-layouts: 36.4 us -> 40.6 us
    all_gather x2 -> x0, waiting for transfers between devices: 95.9 us -> none  [shards(): full_blocks = lax.all_gather(own_blocks, 'cent', axis=1, tiled=True)]
    all_to_all x1, waiting for transfers between devices: 41.4 us -> 92.4 us  [shards(): lax.all_to_all(outgoing, 'point', split_axis=0, concat_axis=0, tiled=True)]
    all_to_all x0 -> x2, blocking collectives: none -> 41.2 us  [the longest x1 31.8 us: shards(): lax.all_to_all(jnp.stack([own_blocks] * lax.axis_size('cent')), 'cent', 0...]
    all_to_all x1, waiting for transfers between devices: 0.01 us -> 16.3 us  [shards(): lax.all_to_all(jnp.stack([own_blocks] * lax.axis_size('cent')), 'cent', 0...]
    unnamed x2, blocking collectives: 80.7 us -> 73.6 us
  transfers between devices with their start and end apart: 6 -> 4, of which waited for: 5 -> 4; matrix products, arithmetic and copies ran while one was open for 6% -> 6% of each run, Pallas kernels for 0% -> 0%
where the time goes in v1:
time: 417 us; the launch traced here: 416 us
  waiting for transfers between devices  176 us (42%)
  blocking collectives  115 us (28%)
  local copies, waits for them, and re-layouts  40.6 us (10%)
  matrix products  28.3 us (7%)
  other arithmetic  28.1 us (7%)
  between operations  14.9 us (4%)
  starting transfers between devices  13.3 us (3%)
    all_to_all x1, waiting for transfers between devices, shards(): lax.all_to_all(outgoing, 'point', split_axis=0, concat_axis=0, tiled=True)  92.4 us
    unnamed x2, blocking collectives  73.6 us
    reduce_scatter x2, waiting for transfers between devices, shards(): lax.psum_scatter(totals, 'cent', scatter_dimension=1, tiled=True)  67.5 us
    all_to_all x1, blocking collectives, shards(): lax.all_to_all(jnp.stack([own_blocks] * lax.axis_size('cent')), 'cent', 0...  31.8 us
    all_to_all x1, waiting for transfers between devices, shards(): lax.all_to_all(jnp.stack([own_blocks] * lax.axis_size('cent')), 'cent', 0...  16.3 us
    scatter x1, local copies, waits for them, and re-layouts, shards(): jnp.zeros((cluster_total * capacity, feature_width), jnp.bfloat16)  15.2 us
    scatter x1, local copies, waits for them, and re-layouts, shards(): occupied = jnp.zeros((cluster_total * capacity,), jnp.bfloat16).at[target...  14.6 us
    dot_general x2, matrix products, responsibilities(): jnp.einsum('pjck,pjcd->jkd', weights.astype(jnp.bfloat16), received, pref...  14.2 us
  transfers between devices with their start and end apart: 4, of which 4 were waited for; matrix products, arithmetic and copies ran while one was open for 6% of the time, Pallas kernels for 0%

profile of v1, /device:TPU:0, one launch (start us, length us, event | category | flops | bytes accessed | tf_op | source)
XLA Modules:
  0.0 416.2 jit_solution(3834331454172118)
XLA Ops:
  7.2 0.8 select_reduce_fusion
  8.0 9.1 %reduce-window.6 = s32[32,16,128]{2,1,0:T(8,128)S(1)} reduce-window(s32[32,16,128]{2,1,0:T(8,128)S(1)} %fusion.37, s32[]{:T(128)} %constant.11.clone.1), window={size=1x1x128 pad=0_0x0_0x127_0}, to_apply=%region_1.2 | reduce-window | flops 8323072 | bytes 524292 | tf_op jit(solution)/shard_map/reduce-window
  17.1 0.1 slice.8
  17.2 0.2 copy.81
  17.5 0.2 reduce-window.9
  17.7 0.1 broadcast_add_fusion
  17.8 0.1 fusion.36
  18.0 14.6 %scatter_custom_fusion.1 = bf16[4096]{0:T(1024)(128)(2,1)S(1)} fusion(s32[2048]{0:T(1024)S(1)} %bitcast.87, bf16[2048]{0:T(1024)(128)(2,1)S(1)} %broadcast.93, bf16[]{:T(256)} %constant.10.clone.1), kind=kCustom, calls=%fused_computation.55 | custom fusion | bytes 8194 | tf_op jit(solution)/shard_map/scatter | solution.py:51
  32.6 0.5 broadcast.115
  33.1 0.7 reduce.2
  33.8 9.5 %all_to_all.25 = bf16[8,2,256]{2,1,0:T(2,128)(2,1)S(1)} all-to-all(bf16[8,2,256]{2,1,0:T(2,128)(2,1)S(1)} %reshape.149), channel_id=1, replica_groups=mesh['point'=8,'cent'=16] {'point'}, dimensions={0} | all-to-all | bytes 16384 | tf_op jit(solution)/shard_map/all_to_all | solution.py:57
  43.3 2.5 stack.4
  45.8 8.0 %all-to-all-start.1 = ((bf16[16,4,16,1024]{3,2,1,0:T(8,128)(2,1)}), bf16[16,4,16,1024]{3,2,1,0:T(8,128)(2,1)S(1)}, u32[]{:S(2)}, u32[]{:S(2)}) async-start(bf16[16,4,16,1024]{3,2,1,0:T(8,128)(2,1)} %stack.4), calls=%async_computation.1 | async-start | bytes 4194304 | tf_op jit(solution)/shard_map/all_to_all | solution.py:65
  53.9 15.2 %scatter_custom_fusion = bf16[4096,1024]{1,0:T(8,128)(2,1)} fusion(s32[2048]{0:T(1024)S(1)} %bitcast.88, bf16[2048,1024]{1,0:T(8,128)(2,1)} %param.4, bf16[]{:T(256)} %constant.10.clone.1), kind=kCustom, calls=%fused_computation.26 | custom fusion | bytes 8389120 | tf_op jit(solution)/shard_map/scatter | solution.py:46
  69.1 16.3 %all-to-all-done.1 = bf16[16,4,16,1024]{3,2,1,0:T(8,128)(2,1)S(1)} async-done(((bf16[16,4,16,1024]{3,2,1,0:T(8,128)(2,1)}), bf16[16,4,16,1024]{3,2,1,0:T(8,128)(2,1)S(1)}, u32[]{:S(2)}, u32[]{:S(2)}) %all-to-all-start.1) | async-done | bytes 2097184 | tf_op jit(solution)/shard_map/all_to_all | solution.py:65
  85.5 5.1 %all-to-all-start = ((bf16[8,512,1024]{2,1,0:T(8,128)(2,1)}), bf16[8,512,1024]{2,1,0:T(8,128)(2,1)}, u32[]{:S(2)}, u32[]{:S(2)}) async-start(bf16[8,512,1024]{2,1,0:T(8,128)(2,1)} %bitcast.77), calls=%async_computation | async-start | bytes 16777216 | tf_op jit(solution)/shard_map/all_to_all | solution.py:56
  90.6 0.0 reduce-scatter.5.cloned.1.call-start
  90.7 1.5 copy.61
  92.2 0.5 multiply_reduce_fusion.1
  92.7 0.1 mul.69
  92.8 92.4 %all-to-all-done = bf16[8,512,1024]{2,1,0:T(8,128)(2,1)} async-done(((bf16[8,512,1024]{2,1,0:T(8,128)(2,1)}), bf16[8,512,1024]{2,1,0:T(8,128)(2,1)}, u32[]{:S(2)}, u32[]{:S(2)}) %all-to-all-start) | async-done | bytes 8388640 | tf_op jit(solution)/shard_map/all_to_all | solution.py:56
  185.2 6.3 %fusion.8 = f32[4,8,128,256]{3,2,1,0:T(8,128)S(1)} fusion(bf16[4,256,1024,1]{2,1,3,0:T(8,128)(2,1)} %bitcast.80, bf16[8,4,128,1024]{3,2,1,0:T(8,128)(2,1)} %bitcast.7), kind=kOutput, calls=%fused_computation.10 | convolution fusion | flops 2147483648 | bytes 14680064 | tf_op jit(solution)/shard_map/pjcd,jkd->pjck/dot_general | solution.py:13
  191.6 1.8 fusion.42
  193.3 0.0 copy-start
  193.4 1.9 copy-done
  195.3 7.1 %fusion.20 = f32[4,256,1024]{2,1,0:T(8,128)} fusion(bf16[8,4,128,1024]{3,2,1,0:T(8,128)(2,1)} %bitcast.7, f32[8,4,128,256]{3,2,0,1:T(8,128)S(1)} %get-tuple-element.5, f32[8,4,128]{2,0,1:T(8,128)S(1)} %bitcast_convert_fusion, f32[8,4,128]{2,0,1:T(8,128)S(1)} %get-tuple-element.4), kind=kOutput, calls=%fused_computation.28 | convolution fusion | flops 2150629376 | bytes 16809984 | tf_op jit(solution)/shard_map/pjck,pjcd->jkd/dot_general | solution.py:18
  202.4 0.0 copy-start.3
  202.4 0.0 copy-start.2
  202.4 0.0 reduce-scatter.5.cloned.1.call-update
  202.4 0.0 reduce-scatter.7.cloned.1.call-start
  202.5 0.6 copy-done.3
  203.1 0.6 dynamic-slice
  204.3 2.9 fusion.32
  207.2 36.5 %all-reduce = f32[4,256]{1,0:T(4,128)S(1)} all-reduce(f32[4,256]{1,0:T(4,128)S(1)} %fusion.32), channel_id=3, replica_groups=mesh['point'=8,'cent'=16] {'cent'}, use_global_device_ids=true, to_apply=%region_11.12.clone | all-reduce | flops 1024 | bytes 8192
  243.7 0.1 dynamic-slice_add_fusion
  243.8 32.7 %reduce-scatter.5.cloned.1.call-done = f32[4,16,1024]{2,1,0:T(8,128)} async-done(((f32[4,256,1024]{2,1,0:T(8,128)}), f32[4,16,1024]{2,1,0:T(8,128)}) %reduce-scatter.5.cloned.1.call-update) | async-done | bytes 262160 | tf_op jit(solution)/shard_map/reduce_scatter | solution.py:69
  276.5 0.0 copy-done.2
  276.5 1.0 divide_convert_fusion.1
  277.5 0.3 stack.5
  277.8 31.8 %all_to_all.26 = bf16[16,4,16,1024]{3,2,1,0:T(8,128)(2,1)S(1)} all-to-all(bf16[16,4,16,1024]{3,2,1,0:T(8,128)(2,1)S(1)} %stack.5), channel_id=1, replica_groups=mesh['point'=8,'cent'=16] {'cent'}, dimensions={0} | all-to-all | bytes 4194304 | tf_op jit(solution)/shard_map/all_to_all | solution.py:65
  309.5 0.3 copy.68
  309.8 7.7 %fusion.4 = f32[4,256,8,128]{1,3,2,0:T(8,128)} fusion(bf16[4,256,1024,1]{2,1,3,0:T(8,128)(2,1)S(1)} %bitcast.81, bf16[8,4,128,1024]{3,2,1,0:T(8,128)(2,1)} %bitcast.7), kind=kOutput, calls=%fused_computation.6 | convolution fusion | flops 2147483648 | bytes 14680064 | tf_op jit(solution)/shard_map/pjcd,jkd->pjck/dot_general | solution.py:13
  317.6 0.5 multiply_reduce_fusion
  318.1 0.1 mul.75
  318.2 5.1 %fusion.43 = (f32[8,4,128]{2,0,1:T(8,128)S(1)}, f32[8,4,128,256]{3,2,0,1:T(8,128)S(1)}) fusion(f32[4,256,8,128]{1,3,2,0:T(8,128)} %fusion.4, f32[4,256]{1,0:T(4,128)S(1)} %mul.75), kind=kOutput, calls=%fused_computation.63 | output fusion | flops 6291711 | bytes 8409088 | tf_op jit(solution)/shard_map/sub | solution.py:17
  323.2 0.0 copy-start.1
  323.2 1.9 copy-done.1
  325.2 7.1 %fusion.23 = f32[4,256,1024]{2,1,0:T(8,128)} fusion(bf16[8,4,128,1024]{3,2,1,0:T(8,128)(2,1)} %bitcast.7, f32[8,4,128,256]{3,2,0,1:T(8,128)S(1)} %get-tuple-element.7, f32[8,4,128]{2,0,1:T(8,128)S(1)} %get-tuple-element.6, f32[8,4,128]{2,0,1:T(8,128)S(1)} %bitcast_convert_fusion), kind=kOutput, calls=%fused_computation.29 | convolution fusion | flops 2150629376 | bytes 16809984 | tf_op jit(solution)/shard_map/pjck,pjcd->jkd/dot_general | solution.py:18
  332.3 0.0 reduce-scatter.7.cloned.1.call-update
  332.3 2.9 fusion.33
  335.2 37.0 %all-reduce.1 = f32[4,256]{1,0:T(4,128)S(1)} all-reduce(f32[4,256]{1,0:T(4,128)S(1)} %fusion.33), channel_id=5, replica_groups=mesh['point'=8,'cent'=16] {'cent'}, use_global_device_ids=true, to_apply=%region_17.18.clone | all-reduce | flops 1024 | bytes 8192
  372.2 0.7 broadcast_add_fusion.1
  372.9 34.8 %reduce-scatter.7.cloned.1.call-done = f32[4,16,1024]{2,1,0:T(8,128)} async-done(((f32[4,256,1024]{2,1,0:T(8,128)}), f32[4,16,1024]{2,1,0:T(8,128)}) %reduce-scatter.7.cloned.1.call-update) | async-done | bytes 262160 | tf_op jit(solution)/shard_map/reduce_scatter | solution.py:69
  407.6 1.7 divide_convert_fusion
  (10 shorter events, 0.1 us)
Async XLA Ops:
  45.8 39.6 %all-to-all-start.1 = ((bf16[16,4,16,1024]{3,2,1,0:T(8,128)(2,1)}), bf16[16,4,16,1024]{3,2,1,0:T(8,128)(2,1)S(1)}, u32[]{:S(2)}, u32[]{:S(2)}) async-start(bf16[16,4,16,1024]{3,2,1,0:T(8,128)(2,1)} %stack.4), calls=%async_computation.1 | async-start | bytes 4194304 | tf_op jit(solution)/shard_map/all_to_all | solution.py:65
  85.5 99.8 %all-to-all-start = ((bf16[8,512,1024]{2,1,0:T(8,128)(2,1)}), bf16[8,512,1024]{2,1,0:T(8,128)(2,1)}, u32[]{:S(2)}, u32[]{:S(2)}) async-start(bf16[8,512,1024]{2,1,0:T(8,128)(2,1)} %bitcast.77), calls=%async_computation | async-start | bytes 16777216 | tf_op jit(solution)/shard_map/all_to_all | solution.py:56
  90.6 185.9 %reduce-scatter.5.cloned.1.call-start = ((), (), s32[]{:S(2)}) async-start(), calls=%async_computation.6 | async-start | bytes 4456448 | tf_op jit(solution)/shard_map/reduce_scatter | solution.py:69
  193.3 2.0 copy-start
  202.4 0.7 copy-start.3
  202.4 74.1 %copy-start.2 = (bf16[4,16,1024]{2,1,0:T(8,128)(2,1)S(1)}, bf16[4,16,1024]{2,1,0:T(8,128)(2,1)}, u32[]{:S(2)}) copy-start(bf16[4,16,1024]{2,1,0:T(8,128)(2,1)} %param.7) | copy-start | bytes 393220
  202.4 205.2 %reduce-scatter.7.cloned.1.call-start = ((), (), s32[]{:S(2)}) async-start(), calls=%async_computation.7 | async-start | bytes 4456448 | tf_op jit(solution)/shard_map/reduce_scatter | solution.py:69
  323.2 2.0 copy-start.1
Sparse Core Ops, SparseCore 0:
  202.6 73.8 reduce-scatter.4
  332.4 75.1 reduce-scatter.6
